TPU v7x, 32 devices: a whole 2x2x4 slice. The times are simulated.
32 devices in a mesh: groups: 2 (over y), block: 16 (over z, x, core).
Axes of the slice: x: 2, y: 2, z: 4, core: 2. Of those that a mesh axis runs over, the one named last changes fastest.
Arguments:
- queries: bfloat16 [49152, 1024], P(('groups', 'block')), parts along dimension 0, may hold values from -6 to 6
- keys: bfloat16 [49152, 1024], P(('groups', 'block')), parts along dimension 0, may hold values from -16 to 16
- values: bfloat16 [49152, 1024], P(('groups', 'block')), parts along dimension 0, may hold values from -12 to 12
Outputs:
- attended: bfloat16 [49152, 1024], P(('groups', 'block')), parts along dimension 0
There are 2 independent parts, one for each index of `groups`. A program takes and returns all parts, laid end to end along the dimension named above; each array names one. Nothing has to cross between parts.
All inputs are finite; a program needn't handle non-finite values.
Results may differ from a plain program's by a relative error of at most 0.0029.
Values sent between devices are 32-bit elements; how exact they have to be, the bound alone decides.
A program may use at most 128 MiB of HBM per device.

v0:
```python
import jax
import jax.numpy as jnp
from jax import lax
from jax.sharding import PartitionSpec as P

HEADS = 8
HEAD_DIM = 128
SPAN = 128


def features(x):
    return (jax.nn.elu(x.astype(jnp.float32)) + 1.0).astype(jnp.bfloat16)


def per_device(queries, keys, values):
    rows = queries.shape[0]
    count = rows // SPAN
    fq = features(queries).reshape(count, SPAN, HEADS, HEAD_DIM)
    fk = features(keys).reshape(count, SPAN, HEADS, HEAD_DIM)
    vv = values.reshape(count, SPAN, HEADS, HEAD_DIM)
    span_state = jnp.einsum("nchd,nche->nhde", fk, vv, preferred_element_type=jnp.float32)
    span_norm = jnp.sum(fk.astype(jnp.float32), axis=1)
    total = jnp.sum(span_state, axis=0)
    total_norm = jnp.sum(span_norm, axis=0)
    devices_n = lax.axis_size("block")
    state_len = HEADS * HEAD_DIM * HEAD_DIM
    flat_len = state_len + HEADS * HEAD_DIM
    width = (flat_len + 128 * devices_n - 1) // (128 * devices_n) * 128
    flat = jnp.concatenate([total.reshape(-1), total_norm.reshape(-1)])
    flat = jnp.pad(flat, (0, width * devices_n - flat_len)).reshape(devices_n, width)
    landed = lax.all_to_all(flat, "block", split_axis=0, concat_axis=0, tiled=True)
    earlier = jnp.cumsum(landed, axis=0) - landed
    returned = lax.all_to_all(earlier, "block", split_axis=0, concat_axis=0, tiled=True).reshape(-1)
    before = returned[:state_len].reshape(HEADS, HEAD_DIM, HEAD_DIM)
    before_norm = returned[state_len:flat_len].reshape(HEADS, HEAD_DIM)
    running = jnp.cumsum(span_state, axis=0) - span_state + before[None]
    running_norm = jnp.cumsum(span_norm, axis=0) - span_norm + before_norm[None]
    inter = jnp.einsum(
        "nchd,nhde->nche", fq, running.astype(jnp.bfloat16), preferred_element_type=jnp.float32
    )
    den_inter = jnp.einsum("nchd,nhd->nch", fq.astype(jnp.float32), running_norm)
    causal = jnp.arange(SPAN)[:, None] >= jnp.arange(SPAN)[None, :]
    scores = jnp.einsum("nchd,nkhd->nhck", fq, fk, preferred_element_type=jnp.float32)
    scores = jnp.where(causal[None, None], scores, jnp.float32(0.0))
    intra = jnp.einsum(
        "nhck,nkhe->nche", scores.astype(jnp.bfloat16), vv, preferred_element_type=jnp.float32
    )
    den = den_inter + jnp.transpose(jnp.sum(scores, axis=-1), (0, 2, 1))
    attended = ((inter + intra) / den[..., None]).astype(jnp.bfloat16)
    return attended.reshape(rows, HEADS * HEAD_DIM)


def solution(mesh):
    placed = (
        P(("groups", "block"), None),
        P(("groups", "block"), None),
        P(("groups", "block"), None),
    )
    return jax.shard_map(
        per_device,
        mesh=mesh,
        in_specs=placed,
        out_specs=P(("groups", "block"), None),
        check_vma=False,
    )
```

profile of v0, /device:TPU:0, one launch (start us, length us, event | category | flops | bytes accessed | tf_op | source)
XLA Modules:
  0.0 79.0 jit_solution(7393231382330989808)
XLA Ops:
  0.0 2.9 %copy.30 = bf16[192,8,8,128]{3,2,1,0:T(8,128)(2,1)S(1)} copy(bf16[192,8,8,128]{3,1,2,0:T(8,128)(2,1)} %bitcast.54) | data formatting | bytes 6291456
  2.9 3.1 %convert_reduce_fusion.1 = (f32[1024]{0:T(1024)S(1)}, bf16[192,8,8,128]{3,1,2,0:T(8,128)(2,1)S(1)}) fusion(bf16[1536,1024]{1,0:T(8,128)(2,1)S(1)} %copy-done.4), kind=kLoop, calls=%fused_computation.16 | loop fusion | flops 12581888 | bytes 6295552 | tf_op jit(solution)/shard_map/reduce_sum | solution.py:24
  6.0 0.8 %copy.29 = bf16[192,8,8,128]{3,2,1,0:T(8,128)(2,1)S(1)} copy(bf16[192,8,8,128]{3,1,2,0:T(8,128)(2,1)S(1)} %get-tuple-element.6) | data formatting | bytes 6291456
  6.8 4.0 %fusion.23 = (f32[8,128,128]{2,1,0:T(8,128)S(1)}, f32[12,8,128,128]{3,2,1,0:T(8,128)}) fusion(bf16[12,128,8,128]{3,2,1,0:T(8,128)(2,1)S(1)} %bitcast.50, bf16[12,128,8,128]{3,2,1,0:T(8,128)(2,1)S(1)} %bitcast.47), kind=kOutput, calls=%fused_computation.41 | convolution fusion | flops 404094976 | bytes 13107200 | tf_op jit(solution)/shard_map/nchd,nche->nhde/dot_general | solution.py:21
  10.8 0.8 %select_maximum_fusion = f32[133120]{0:T(1024)} fusion(f32[1024]{0:T(1024)S(1)} %get-tuple-element.5, f32[131072]{0:T(1024)S(1)} %bitcast.56), kind=kLoop, calls=%fused_computation.35 | loop fusion | flops 532480 | bytes 1060864 | tf_op jit(solution)/shard_map/concatenate | solution.py:29
  11.7 7.4 %all-to-all-start = ((f32[16,1,8320]{2,1,0:T(1,128)}), f32[16,1,8320]{2,1,0:T(1,128)}, u32[]{:S(2)}, u32[]{:S(2)}) async-start(f32[16,1,8320]{2,1,0:T(1,128)} %bitcast.55), calls=%async_computation | async-start | bytes 1064960 | tf_op jit(solution)/shard_map/all_to_all | solution.py:31
  19.1 4.7 %fusion.10 = bf16[192,8,8,128]{3,1,2,0:T(8,128)(2,1)S(1)} fusion(bf16[1536,1024]{1,0:T(8,128)(2,1)} %param.3), kind=kLoop, calls=%fused_computation.21 | loop fusion | flops 9437184 | bytes 6291456
  23.8 2.5 %copy.31 = bf16[192,8,8,128]{3,2,1,0:T(8,128)(2,1)} copy(bf16[192,8,8,128]{3,1,2,0:T(8,128)(2,1)S(1)} %fusion.10) | data formatting | bytes 6291456
  26.3 4.9 %copy.27 = bf16[12,128,8,128]{1,3,2,0:T(8,128)(2,1)} copy(bf16[12,128,8,128]{3,2,1,0:T(8,128)(2,1)} %bitcast.52) | data formatting | bytes 6291456 | tf_op jit(solution)/shard_map/reshape | solution.py:18
  31.2 0.4 convert_reduce_fusion
  31.7 1.5 %copy-done.2 = bf16[12,128,8,128]{1,3,2,0:T(8,128)(2,1)S(1)} copy-done((bf16[12,128,8,128]{1,3,2,0:T(8,128)(2,1)S(1)}, bf16[12,128,8,128]{1,3,2,0:T(8,128)(2,1)}, u32[]{:S(2)}) %copy-start.2) | copy-done | bytes 3145752
  33.1 2.9 %select_reduce_fusion = (f32[12,8,128]{2,1,0:T(8,128)S(1)}, bf16[12,8,128,128]{2,3,1,0:T(8,128)(2,1)}) fusion(pred[128,128]{0,1:T(8,128)(4,1)S(1)} %iota_compare_fusion.1, bf16[12,128,8,128]{1,3,2,0:T(8,128)(2,1)S(1)} %copy-done.2, bf16[12,128,8,128]{3,2,1,0:T(8,128)(2,1)S(1)} %bitcast.49), kind=kOutput, calls=%fused_computation.17 | convolution fusion | flops 407359488 | bytes 9502720 | tf_op jit(solution)/shard_map/nchd,nkhd->nhck/dot_general | solution.py:43
  36.0 2.6 %reduce-window_subtract_fusion = f32[16,1,8320]{2,1,0:T(1,128)} fusion(f32[16,1,8320]{2,1,0:T(1,128)} %all-to-all-done), kind=kOutput, calls=%fused_computation.4 | output fusion | flops 2129920 | bytes 1064960 | tf_op jit(solution)/shard_map/jit(cumsum)/reduce_window_sum | solution.py:32
  38.5 6.0 %all-to-all-start.1 = ((f32[16,1,8320]{2,1,0:T(1,128)}), f32[16,1,8320]{2,1,0:T(1,128)}, u32[]{:S(2)}, u32[]{:S(2)}) async-start(f32[16,1,8320]{2,1,0:T(1,128)} %reduce-window_subtract_fusion), calls=%async_computation.1 | async-start | bytes 1064960 | tf_op jit(solution)/shard_map/all_to_all | solution.py:33
  44.6 6.7 %fusion.24 = f32[12,8,128,128]{3,2,1,0:T(8,128)} fusion(f32[12,8,128,128]{3,2,1,0:T(8,128)} %get-tuple-element.8), kind=kOutput, calls=%fused_computation.42 | output fusion | flops 17301504 | bytes 12582912 | tf_op jit(solution)/shard_map/jit(cumsum)/reduce_window_sum | solution.py:36
  51.3 3.8 %fusion.8 = f32[12,8,128,128]{2,3,1,0:T(8,128)} fusion(bf16[12,8,128,128]{2,3,1,0:T(8,128)(2,1)S(1)} %copy-done.5, pred[128,128]{0,1:T(8,128)(4,1)S(1)} %iota_compare_fusion.1, bf16[12,128,8,128]{3,2,1,0:T(8,128)(2,1)S(1)} %bitcast.51), kind=kOutput, calls=%fused_computation.19 | convolution fusion | flops 404226048 | bytes 12599296 | tf_op jit(solution)/shard_map/nhck,nkhe->nche/dot_general | solution.py:45
  55.1 4.1 %all-to-all-done.1 = f32[16,1,8320]{2,1,0:T(1,128)} async-done(((f32[16,1,8320]{2,1,0:T(1,128)}), f32[16,1,8320]{2,1,0:T(1,128)}, u32[]{:S(2)}, u32[]{:S(2)}) %all-to-all-start.1) | async-done | bytes 532512 | tf_op jit(solution)/shard_map/all_to_all | solution.py:33
  59.2 0.7 slice_bitcast_fusion
  59.9 0.1 fusion.20
  60.0 0.9 %fusion.25 = f32[12,8,1,128]{3,2,1,0:T(1,128)S(1)} fusion(f32[12,8,128,1]{2,3,1,0:T(1,128)S(1)} %bitcast.59, bf16[12,128,8,128]{1,3,2,0:T(8,128)(2,1)S(1)} %copy-done.3), kind=kOutput, calls=%fused_computation.43 | convolution fusion | flops 3145728 | bytes 3244032 | tf_op jit(solution)/shard_map/nchd,nhd->nch/dot_general | solution.py:41
  61.0 1.9 %slice.12 = f32[131072]{0:T(1024)} slice(f32[133120]{0:T(1024)} %bitcast.2), slice={[0:131072]} | slice | bytes 1048576 | tf_op jit(solution)/shard_map/slice | solution.py:34
  62.8 10.1 %fusion.7 = bf16[12,128,8,128]{1,3,2,0:T(8,128)(2,1)} fusion(f32[12,8,128,128]{2,3,1,0:T(8,128)} %fusion.8, f32[12,128,8]{1,2,0:T(8,128)S(1)} %add_bitcast_fusion, bf16[12,128,8,128]{1,3,2,0:T(8,128)(2,1)S(1)} %copy-done.3, f32[12,8,128,128]{3,2,1,0:T(8,128)} %fusion.24, f32[12,8,128,128]{3,2,1,0:T(8,128)} %get-tuple-element.8, f32[8,128,128]{2,1,0:T(8,128)} %bitcast.57), kind=kOutput, calls=%fused_computation.13 | convolution fusion | flops 412090368 | bytes 25739264 | tf_op jit(solution)/shard_map/nchd,nhde->nche/dot_general | solution.py:38
  72.9 3.6 %copy.22 = bf16[12,128,8,128]{3,2,1,0:T(8,128)(2,1)S(1)} copy(bf16[12,128,8,128]{1,3,2,0:T(8,128)(2,1)} %fusion.7) | data formatting | bytes 6291456 | tf_op jit(solution)/shard_map/convert_element_type | solution.py:49
  76.5 2.5 %copy.48 = bf16[192,8,8,128]{3,1,2,0:T(8,128)(2,1)} copy(bf16[192,8,8,128]{3,2,1,0:T(8,128)(2,1)S(1)} %bitcast.53) | data formatting | bytes 6291456
  (14 shorter events, 0.0 us)
Async XLA Ops:
  0.0 2.9 %copy-start.4 = (bf16[1536,1024]{1,0:T(8,128)(2,1)S(1)}, bf16[1536,1024]{1,0:T(8,128)(2,1)}, u32[]{:S(2)}) copy-start(bf16[1536,1024]{1,0:T(8,128)(2,1)} %param.4) | copy-start | bytes 9437188
  2.9 3.9 %copy-start = (bf16[192,8,8,128]{3,2,1,0:T(8,128)(2,1)}, bf16[192,8,8,128]{3,2,1,0:T(8,128)(2,1)S(1)}, u32[]{:S(2)}) copy-start(bf16[192,8,8,128]{3,2,1,0:T(8,128)(2,1)S(1)} %copy.30) | copy-start | bytes 9437188
  11.7 24.3 %all-to-all-start = ((f32[16,1,8320]{2,1,0:T(1,128)}), f32[16,1,8320]{2,1,0:T(1,128)}, u32[]{:S(2)}, u32[]{:S(2)}) async-start(f32[16,1,8320]{2,1,0:T(1,128)} %bitcast.55), calls=%async_computation | async-start | bytes 1064960 | tf_op jit(solution)/shard_map/all_to_all | solution.py:31
  31.2 1.9 %copy-start.2 = (bf16[12,128,8,128]{1,3,2,0:T(8,128)(2,1)S(1)}, bf16[12,128,8,128]{1,3,2,0:T(8,128)(2,1)}, u32[]{:S(2)}) copy-start(bf16[12,128,8,128]{1,3,2,0:T(8,128)(2,1)} %copy.27) | copy-start | bytes 9437188
  38.5 20.7 %all-to-all-start.1 = ((f32[16,1,8320]{2,1,0:T(1,128)}), f32[16,1,8320]{2,1,0:T(1,128)}, u32[]{:S(2)}, u32[]{:S(2)}) async-start(f32[16,1,8320]{2,1,0:T(1,128)} %reduce-window_subtract_fusion), calls=%async_computation.1 | async-start | bytes 1064960 | tf_op jit(solution)/shard_map/all_to_all | solution.py:33
  44.6 6.7 %copy-start.1 = (bf16[192,8,8,128]{3,2,1,0:T(8,128)(2,1)S(1)}, bf16[192,8,8,128]{3,2,1,0:T(8,128)(2,1)}, u32[]{:S(2)}) copy-start(bf16[192,8,8,128]{3,2,1,0:T(8,128)(2,1)} %copy-done) | copy-start | bytes 9437188
  44.6 6.7 %copy-start.5 = (bf16[12,8,128,128]{2,3,1,0:T(8,128)(2,1)S(1)}, bf16[12,8,128,128]{2,3,1,0:T(8,128)(2,1)}, u32[]{:S(2)}) copy-start(bf16[12,8,128,128]{2,3,1,0:T(8,128)(2,1)} %get-tuple-element.10) | copy-start | bytes 9437188
  51.3 8.8 %copy-start.3 = (bf16[12,128,8,128]{1,3,2,0:T(8,128)(2,1)S(1)}, bf16[12,128,8,128]{1,3,2,0:T(8,128)(2,1)}, u32[]{:S(2)}) copy-start(bf16[12,128,8,128]{1,3,2,0:T(8,128)(2,1)} %copy.27) | copy-start | bytes 9437188
where the time goes:
time: 79.6 us; the launch traced here: 79 us
  matrix products  21.7 us (27%)
  local copies, waits for them, and re-layouts  21.2 us (27%)
  other arithmetic  18.4 us (23%)
  starting transfers between devices  13.4 us (17%)
  waiting for transfers between devices  4.14 us (5%)
    unnamed x16, local copies, waits for them, and re-layouts  10.1 us
    dot_general x1, matrix products, per_device(): jnp.einsum('nchd,nhde->nche', fq, running.astype(jnp.bfloat16), preferred...  10.1 us
    all_to_all x1, starting transfers between devices, per_device(): lax.all_to_all(flat, 'block', split_axis=0, concat_axis=0, tiled=True)  7.41 us
    another operation x1, other arithmetic, per_device(): running = jnp.cumsum(span_state, axis=0) - span_state + before[None]  6.7 us
    all_to_all x1, starting transfers between devices, per_device(): lax.all_to_all(earlier, 'block', split_axis=0, concat_axis=0, tiled=True)  6.01 us
    reshape x1, local copies, waits for them, and re-layouts, per_device(): fq = features(queries).reshape(count, SPAN, HEADS, HEAD_DIM)  4.92 us
    unnamed x1, other arithmetic  4.73 us
    all_to_all x1, waiting for transfers between devices, per_device(): lax.all_to_all(earlier, 'block', split_axis=0, concat_axis=0, tiled=True)  4.13 us
  transfers between devices with their start and end apart: 2, of which 1 were waited for; matrix products, arithmetic and copies ran while one was open for 33% of the time, Pallas kernels for 0%

commit v1 on v0

v1 whole, which is shorter than its diff:
```python
import functools

import jax
import jax.numpy as jnp
from jax import lax
from jax.experimental import pallas as pl
from jax.experimental.pallas import tpu as pltpu
from jax.sharding import PartitionSpec as P

HEADS = 8
DIM = 128
TILE = 256
HALF = TILE // 2
F32 = jnp.float32
BF16 = jnp.bfloat16


def features(x):
    x = x.astype(F32)
    return jnp.where(x > 0.0, x + 1.0, jnp.exp(x)).astype(BF16)


def nt(a, b):
    return lax.dot_general(a, b, (((1,), (1,)), ((), ())), preferred_element_type=F32)


def tn(a, b):
    return lax.dot_general(a, b, (((0,), (0,)), ((), ())), preferred_element_type=F32)


def nn(a, b):
    return jnp.dot(a, b, preferred_element_type=F32)


def kernel(
    n, q_hbm, k_hbm, v_hbm, o_hbm, qb, kb, vb, ob, num, den, kvt, ksum,
    give, got, back, before, in_sem, out_sem, s1, r1, s2, r2,
):
    rows = qb.shape[1]
    tiles = rows // TILE
    piece = HEADS * DIM // n
    per_head = n // HEADS
    me = lax.axis_index("block")

    def cols(h):
        return pl.ds(pl.multiple_of(h * DIM, DIM), DIM)

    def load(which, src, dst, h):
        return pltpu.make_async_copy(src.at[:, cols(h)], dst.at[h], in_sem.at[which, h])

    def send_total(o, slot):
        return pltpu.make_async_remote_copy(
            src_ref=give.at[o], dst_ref=got.at[slot], send_sem=s1.at[o],
            recv_sem=r1.at[slot], device_id={"block": o},
        )

    def send_back(o, slot):
        return pltpu.make_async_remote_copy(
            src_ref=back.at[o], dst_ref=before.at[slot], send_sem=s2.at[o],
            recv_sem=r2.at[slot], device_id={"block": o},
        )

    def store(h):
        return pltpu.make_async_copy(ob.at[h], o_hbm.at[:, cols(h)], out_sem.at[h])

    for h in range(HEADS):
        load(0, k_hbm, kb, h).start()
        load(1, v_hbm, vb, h).start()
    for h in range(HEADS):
        load(2, q_hbm, qb, h).start()

    barrier = pltpu.get_barrier_semaphore()

    @pl.loop(0, n)
    def _(o):
        @pl.when(o != me)
        def _():
            pl.semaphore_signal(barrier, inc=1, device_id={"block": o})

    def state(h):
        load(0, k_hbm, kb, h).wait()
        load(1, v_hbm, vb, h).wait()
        total = jnp.zeros((DIM, DIM), F32)
        norm = jnp.zeros((8, DIM), F32)
        for t in range(tiles):
            at = pl.ds(t * TILE, TILE)
            fk = features(kb[h, at, :])
            kb[h, at, :] = fk
            kvt[h, t] = total
            ksum[h, t] = norm
            total = total + tn(vb[h, at, :], fk)
            part = jnp.sum(fk.astype(F32).reshape(TILE // 8, 8, DIM), axis=0)
            norm = norm + jnp.broadcast_to(jnp.sum(part, axis=0, keepdims=True), (8, DIM))
        return total, norm

    def share(h, total, norm):
        for j in range(per_head):
            o = h * per_head + j
            give[o, pl.ds(0, piece), :] = total[j * piece : (j + 1) * piece]
            give[o, pl.ds(piece, 8), :] = norm

            @pl.when(o != me)
            def _():
                send_total(o, me).start()

            @pl.when(o == me)
            def _():
                got[me] = give[o]

    total, norm = state(0)
    pl.semaphore_wait(barrier, n - 1)
    share(0, total, norm)

    @pl.loop(1, HEADS)
    def _(h):
        share(h, *state(h))

    later = lax.broadcasted_iota(jnp.int32, (HALF, HALF), 1) > lax.broadcasted_iota(
        jnp.int32, (HALF, HALF), 0
    )
    ones = jnp.ones((TILE, DIM), BF16)

    def local(h):
        load(2, q_hbm, qb, h).wait()
        for t in range(tiles):
            at = pl.ds(t * TILE, TILE)
            fq = features(qb[h, at, :])
            qb[h, at, :] = fq
            fk = kb[h, at, :]
            vo = jnp.concatenate([vb[h, at, :], ones], axis=1)
            top = jnp.where(later, 0.0, nt(fq[:HALF], fk[:HALF])).astype(BF16)
            low = nt(fq[HALF:], fk)
            low = jnp.concatenate(
                [low[:, :HALF].astype(BF16), jnp.where(later, 0.0, low[:, HALF:]).astype(BF16)],
                axis=1,
            )
            r = jnp.concatenate([nn(top, vo[:HALF]), nn(low, vo)], axis=0)
            if t:
                w = jnp.concatenate(
                    [kvt[h, t], jnp.broadcast_to(ksum[h, t][:1], (DIM, DIM))], axis=0
                ).astype(BF16)
                r = r + nt(fq, w)
            num[h, at, :] = r[:, :DIM]
            den[h, at, :] = r[:, DIM:]

    def answer():
        def step(src, acc):
            @pl.when(src != me)
            def _():
                send_total(src, src).wait_recv()

            back[src] = acc

            @pl.when(src != me)
            def _():
                send_back(src, me).start()

            @pl.when(src == me)
            def _():
                before[me] = acc

            return acc + got[src]

        lax.fori_loop(0, n, step, jnp.zeros((piece + 8, DIM), F32))

    split = HEADS // 2

    @pl.loop(0, split)
    def _(h):
        local(h)

    answer()

    @pl.loop(split, HEADS)
    def _(h):
        local(h)

    @pl.loop(0, HEADS)
    def _(h):
        parts = []
        for j in range(per_head):
            o = h * per_head + j

            @pl.when(o != me)
            def _():
                send_back(o, o).wait_recv()

            parts.append(before[o, pl.ds(0, piece), :])
        norm = before[h * per_head, pl.ds(piece, 8), :]
        w = jnp.concatenate(
            parts + [jnp.broadcast_to(norm[:1], (DIM, DIM))], axis=0
        ).astype(BF16)
        for t in range(tiles):
            at = pl.ds(t * TILE, TILE)
            r = nt(qb[h, at, :], w)
            d = den[h, at, :] + r[:, DIM:]
            x = pl.reciprocal(d, approx=True)
            x = x * (2.0 - d * x)
            ob[h, at, :] = ((num[h, at, :] + r[:, :DIM]) * x).astype(BF16)
        store(h).start()

    @pl.loop(0, n)
    def _(o):
        @pl.when(o != me)
        def _():
            send_total(o, me).wait_send()
            send_back(o, me).wait_send()

    @pl.loop(0, HEADS)
    def _(h):
        store(h).wait()


def solution(mesh):
    n = mesh.shape["block"]
    piece = HEADS * DIM // n

    def per_device(q, k, v):
        rows = q.shape[0]
        tiles = rows // TILE
        whole = pltpu.VMEM((HEADS, rows, DIM), BF16)
        wide = pltpu.VMEM((HEADS, rows, DIM), F32)
        slots = pltpu.VMEM((n, piece + 8, DIM), F32)
        line = pltpu.SemaphoreType.DMA((n,))
        return pl.pallas_call(
            functools.partial(kernel, n),
            out_shape=jax.ShapeDtypeStruct(q.shape, BF16),
            in_specs=[pl.BlockSpec(memory_space=pl.ANY)] * 3,
            out_specs=pl.BlockSpec(memory_space=pl.ANY),
            scratch_shapes=[
                whole, whole, whole, whole, wide, wide,
                pltpu.VMEM((HEADS, tiles, DIM, DIM), F32),
                pltpu.VMEM((HEADS, tiles, 8, DIM), F32),
                slots, slots, slots, slots,
                pltpu.SemaphoreType.DMA((3, HEADS)),
                pltpu.SemaphoreType.DMA((HEADS,)),
                line, line, line, line,
            ],
            compiler_params=pltpu.CompilerParams(
                collective_id=0, has_side_effects=True, vmem_limit_bytes=50 * 2**20
            ),
        )(q, k, v)

    spec = P(("groups", "block"), None)
    return jax.shard_map(
        per_device, mesh=mesh, in_specs=(spec,) * 3, out_specs=spec, check_vma=False
    )
```

time: 79.6 us -> 37.5 us (0.47)
  the two profiles are of different devices: /device:TPU:0 before, /device:TPU:31 now
where the time goes in v1:
time: 37.5 us; the launch traced here: 37.4 us
  Pallas kernels  35.7 us (95%)
  local copies, waits for them, and re-layouts  1.67 us (4%)
    pallas_call x1, Pallas kernels, per_device(): pl.pallas_call(functools.partial(kernel, n), out_shape=jax.ShapeDtypeStru...  35.7 us
    unnamed x1, local copies, waits for them, and re-layouts  1.67 us

profile of v1, /device:TPU:31, one launch (start us, length us, event | category | flops | bytes accessed | tf_op | source)
XLA Modules:
  0.0 37.4 jit_solution(4002878595520292439)
XLA Ops:
  0.0 35.7 %shard_map.37 = bf16[1536,1024]{1,0:T(8,128)(2,1)S(1)} custom-call(bf16[1536,1024]{1,0:T(8,128)(2,1)} %q_hbm.1, bf16[1536,1024]{1,0:T(8,128)(2,1)} %k_hbm.1, bf16[1536,1024]{1,0:T(8,128)(2,1)} %v_hbm.1), custom_call_target="tpu_custom_call" | custom-call | tf_op jit(solution)/shard_map/pallas_call | solution.py:225
  35.7 1.7 %copy.5 = bf16[1536,1024]{1,0:T(8,128)(2,1)} copy(bf16[1536,1024]{1,0:T(8,128)(2,1)S(1)} %shard_map.37) | data formatting | bytes 6291456
